TPU v7x, 32 devices: a whole 2x2x4 slice. The times are simulated.
32 devices in a mesh: gx: 8 (over y, x, core), gy: 4 (over z).
Axes of the slice: x: 2, y: 2, z: 4, core: 2. Of those that a mesh axis runs over, the one named last changes fastest.
Arguments:
- velocity: float32 [3, 512, 128, 128], P(None, 'gx', 'gy'), may hold values from -6 to 6
- inflow: float32 [3, 128, 128], P(None, 'gy'), may hold values from -6 to 6
- azimuth: float32 [32], replicated, may hold values from -3.140625 to 3.140625
- positions: int32 [32, 2], replicated, may hold values from 0 to 511, as said below
- crossings: int32 [32, 6], replicated, may hold values from -1 to 95, as said below
- lag_state: float32 [96, 128], P(('gx', 'gy')), may hold values from -0.5 to 1.5
- lag_rate: float32 [96, 128], P(('gx', 'gy')), may hold values from 0.05 to 0.8
- chord_len: float32 [128], replicated, may hold values from 0.3 to 1.5
- twist_angle: float32 [128], replicated, may hold values from -0.4 to 0.4
Outputs:
- velocity_out: float32 [3, 512, 128, 128], P(None, 'gx', 'gy')
- state_out: float32 [96, 128], P(('gx', 'gy'))
Inputs may be any that keep to these rules, and one draw needn't show every extreme that they name: `positions`: every rotor's hub lies in the tile of its cell, 2 or more cells from both x edges of that tile and at most 15 cells below its upper y edge; a tile holds at most two hubs, and two hubs in one tile differ in x. `crossings`: row t lists the blades 3 r, 3 r + 1, 3 r + 2 of every rotor r whose hub lies in tile t, then of some of the rotors whose hub lies in the tile just before t along y (cyclic, same x), and -1 in the remaining entries at the end. Every blade appears in one or two rows; some rows hold 6 blades.
All inputs are finite; a program needn't handle non-finite values.
Results may differ from a plain program's by a relative error of at most 0.0003.
Values sent between devices are 32-bit elements; how exact they have to be, the bound alone decides.
A program may use at most 128 MiB of HBM per device.

v0:
```python
import functools
import math

import jax
import jax.numpy as jnp
from jax import lax
from jax.experimental import pallas as pl
from jax.experimental.pallas import tpu as pltpu
from jax.sharding import PartitionSpec as P

RADIUS = 12
HUB = 15
STEPS = 2
EPSILON = 2.0
SUPPORT = 3.0
TURN_RATE = 0.1
SPIN = 0.25
LIFT_SLOPE = 2.0 * math.pi
FORCE_SCALE = 0.15
ADVECT = 0.5
DIFFUSE = 0.05
PRECISE = lax.Precision.HIGHEST
MESH = pl.DeviceIdType.MESH
BLADES = 3
ENTRIES = 2
ROWS = 8
CHUNKS = 3
UNROLL = 4


def taper_const(distance):
    square = distance * distance
    term = max(1.0 - square / (SUPPORT * SUPPORT), 0.0)
    return math.exp(-square / EPSILON**2) * term * term / (EPSILON * math.sqrt(math.pi))


KERN_X = [taper_const(float(i)) for i in range(3)]


def taper_kernel(distance):
    square = distance * distance
    term = jnp.maximum(1.0 - square * (1.0 / (SUPPORT * SUPPORT)), 0.0)
    return (
        jnp.exp(square * (-1.0 / (EPSILON * EPSILON)))
        * (term * term)
        * (1.0 / (EPSILON * math.sqrt(math.pi)))
    )


def weight_x(offset):
    dist = jnp.abs(offset)
    return jnp.where(
        dist == 0,
        KERN_X[0],
        jnp.where(dist == 1, KERN_X[1], jnp.where(dist == 2, KERN_X[2], 0.0)),
    ).astype(jnp.float32)


def farm_kernel(
    nx,
    ny,
    vel_hbm,
    inflow_hbm,
    az_hbm,
    pos_hbm,
    cross_hbm,
    lag_hbm,
    rate_hbm,
    chord_hbm,
    twist_hbm,
    out_hbm,
    state_hbm,
    inflow_ref,
    az_ref,
    pos_ref,
    cross_ref,
    lag_ref,
    rate_ref,
    chord_ref,
    twist_ref,
    state_ref,
    small_sem,
    grid0,
    grid1,
    grid2,
    halo_x,
    halo_y,
    face_y,
    part_out,
    part_in,
    kern_y,
    kern_z,
    spread,
    lag_pack,
    lag_g1,
    lag_g2,
    end_pack,
    end_g1,
    end_g2,
    load_sem,
    store_sem,
    hx_send,
    hx_recv,
    hy_send,
    hy_recv,
    ps_send,
    ps_recv,
    gy_send,
    gy_recv,
    gx_send,
    gx_recv,
):
    grids = (grid0, grid1, grid2)
    _, cx2, cy, nz = grid0.shape
    cx = cx2 - 2
    split = cx * 3 // 4
    total_y = cy * ny
    gx = lax.axis_index("gx")
    gy = lax.axis_index("gy")
    tile = gx * ny + gy
    east = lax.rem(gx + 1, nx)
    west = lax.rem(gx + nx - 1, nx)
    up = lax.rem(gy + 1, ny)
    down = lax.rem(gy + ny - 1, ny)

    load = pltpu.make_async_copy(vel_hbm, grid0.at[:, pl.ds(1, cx)], load_sem)
    smalls = [
        pltpu.make_async_copy(source, target, small_sem.at[i])
        for i, (source, target) in enumerate(
            (
                (az_hbm, az_ref),
                (pos_hbm, pos_ref),
                (cross_hbm, cross_ref),
                (lag_hbm, lag_ref),
                (rate_hbm, rate_ref),
                (chord_hbm, chord_ref),
                (twist_hbm, twist_ref),
                (inflow_hbm, inflow_ref),
            )
        )
    ]
    for copy in smalls:
        copy.start()
    load.start()

    barrier = pltpu.get_barrier_semaphore()
    for d in range(1, ny):
        pl.semaphore_signal(
            barrier, inc=1, device_id={"gy": lax.rem(gy + d, ny)}, device_id_type=MESH
        )
    for d in range(1, nx):
        pl.semaphore_signal(
            barrier, inc=1, device_id={"gx": lax.rem(gx + d, nx)}, device_id_type=MESH
        )

    for copy in smalls:
        copy.wait()

    rotor, hub_x, load_x, shift_y, valid, az = [], [], [], [], [], []
    for e in range(ENTRIES):
        blade = cross_ref[BLADES * e, tile]
        r = jnp.where(blade >= 0, blade, 0) // BLADES
        rotor.append(jnp.where(blade >= 0, r, -1))
        valid.append(jnp.where(blade >= 0, 1.0, 0.0).astype(jnp.float32))
        hub_x.append(jnp.where(blade >= 0, pos_ref[0, r] - gx * cx, 2))
        load_x.append(jnp.clip(hub_x[e], 2, cx - 3))
        off = gy * cy - pos_ref[1, r] + total_y + total_y // 2
        shift_y.append(lax.rem(off, total_y) - total_y // 2)
        az.append(az_ref[r])

    def matches(other):
        found = []
        for f in range(ENTRIES):
            blade = cross_ref[BLADES * f, other]
            found.append(jnp.where(blade >= 0, jnp.where(blade >= 0, blade, 0) // BLADES, -2))
        return [
            [jnp.where(rotor[e] == found[f], 1.0, 0.0).astype(jnp.float32) for f in range(ENTRIES)]
            for e in range(ENTRIES)
        ]

    row = lax.broadcasted_iota(jnp.int32, (ROWS, nz), 0)
    first = row < BLADES
    lane8 = lax.broadcasted_iota(jnp.int32, (ROWS, nz), 1).astype(jnp.float32)
    radius = RADIUS * (lane8 + 0.5) / nz
    spin = jnp.where(first, row, row - BLADES).astype(jnp.float32) * (2.0 * math.pi / 3.0)
    base = jnp.where(first, az[0], az[1])
    mask_rows = []
    for other in (gx * ny + down, gx * ny + up):
        m = matches(other)
        mask_rows.append(
            (jnp.where(first, m[0][0], m[1][1]), jnp.where(first, m[0][1], m[1][0]))
        )
    cos_all, sin_all = [], []
    rows_y = lax.broadcasted_iota(jnp.int32, (cy, nz), 0)
    rows_z = lax.broadcasted_iota(jnp.int32, (nz, nz), 0).astype(jnp.float32) - HUB
    for n in range(STEPS):
        theta = base + TURN_RATE * n + spin
        cos_n, sin_n = jnp.cos(theta), jnp.sin(theta)
        cos_all.append(cos_n)
        sin_all.append(sin_n)
        rc, rs = radius * cos_n, radius * sin_n
        for e in range(ENTRIES):
            y_rel = (rows_y + shift_y[e]).astype(jnp.float32)
            for b in range(BLADES):
                i = BLADES * e + b
                kern_y[n, e, :, b * nz : (b + 1) * nz] = taper_kernel(y_rel - rs[i : i + 1]) * valid[e]
                kern_z[n, e, :, b * nz : (b + 1) * nz] = taper_kernel(rows_z - rc[i : i + 1])
    cos_t, sin_t = jnp.cos(twist_ref[...]), jnp.sin(twist_ref[...])
    chord = FORCE_SCALE * chord_ref[...]

    lag_pack[0:BLADES] = lag_ref[...]
    lag_pack[BLADES : 2 * BLADES] = rate_ref[...]
    lag_pack[2 * BLADES : ROWS] = jnp.zeros((ROWS - 2 * BLADES, nz), jnp.float32)

    pl.semaphore_wait(barrier, nx - 1 + ny - 1)

    started = []

    def send(src, dst, send_sem, recv_sem, axis, peer):
        copy = pltpu.make_async_remote_copy(
            src_ref=src,
            dst_ref=dst,
            send_sem=send_sem,
            recv_sem=recv_sem,
            device_id={axis: peer},
            device_id_type=MESH,
        )
        copy.start()
        started.append(copy)
        return copy

    def gather_start(k, pack, first_level):
        copies = [
            send(pack, first_level.at[gy], gy_send.at[k, d], gy_recv.at[k, d], "gy", lax.rem(gy + d, ny))
            for d in range(1, ny)
        ]
        first_level[gy] = pack[...]
        return copies

    def gather_next(k, copies, first_level, second_level):
        for copy in copies:
            copy.wait_recv()
        copies = [
            send(first_level, second_level.at[gx], gx_send.at[k, d], gx_recv.at[k, d], "gx", lax.rem(gx + d, nx))
            for d in range(1, nx)
        ]
        second_level[gx] = first_level[...]
        return copies

    lag_copies = gather_start(0, lag_pack, lag_g1)
    load.wait()

    lag = None
    rate = None
    zero_rows = jnp.zeros((ROWS - 2 * BLADES, nz), jnp.float32)
    lane = lax.broadcasted_iota(jnp.int32, (cy, nz), 1)
    row_c = lax.broadcasted_iota(jnp.int32, (cy, nz), 0)
    is_first_z, is_last_z = lane == 0, lane == nz - 1
    is_first_y, is_last_y = row_c == 0, row_c == cy - 1
    end_copies = None
    stores = []
    for n in range(STEPS):
        src, dst = grids[n], grids[n + 1]
        sampled = [[], [], []]
        for e in range(ENTRIES):
            field = None
            for i in range(-2, 3):
                term = KERN_X[abs(i)] * src[:, load_x[e] + 1 + i]
                field = term if field is None else field + term
            inner = jnp.dot(
                field.reshape(3 * cy, nz),
                kern_z[n, e],
                precision=PRECISE,
                preferred_element_type=jnp.float32,
            )
            for c in range(3):
                reduced = jnp.sum(inner[c * cy : (c + 1) * cy] * kern_y[n, e], axis=0, keepdims=True)
                sampled[c] += [reduced[:, b * nz : (b + 1) * nz] for b in range(BLADES)]
        for c in range(3):
            part_out[n, c] = jnp.concatenate(sampled[c] + [zero_rows], axis=0)
        part_copies = [
            send(part_out.at[n], part_in.at[n, 0], ps_send.at[n, 0], ps_recv.at[n, 0], "gy", up),
            send(part_out.at[n], part_in.at[n, 1], ps_send.at[n, 1], ps_recv.at[n, 1], "gy", down),
        ]
        halo_copies = [
            send(src.at[:, cx], halo_x.at[n, 0], hx_send.at[n, 0], hx_recv.at[n, 0], "gx", east),
            send(src.at[:, 1], halo_x.at[n, 1], hx_send.at[n, 1], hx_recv.at[n, 1], "gx", west),
        ]

        flat = src.reshape(3 * cx2 * cy, nz)
        for c in range(3):
            start = (c * cx2 + 1) * cy
            face_y[n, 0, c] = flat[pl.ds(start + cy - 1, cx, stride=cy), :]
            face_y[n, 1, c] = flat[pl.ds(start, cx, stride=cy), :]
        halo_copies += [
            send(face_y.at[n, 0], halo_y.at[n, 0], hy_send.at[n, 0], hy_recv.at[n, 0], "gy", up),
            send(face_y.at[n, 1], halo_y.at[n, 1], hy_send.at[n, 1], hy_recv.at[n, 1], "gy", down),
        ]
        if n == 0:
            lag_copies = gather_next(0, lag_copies, lag_g1, lag_g2)

        def halo_rows(c, x):
            return halo_y[n, 0, c, pl.ds(x, 1), :], halo_y[n, 1, c, pl.ds(x, 1), :]

        def moved(c, x, below, above):
            cur = src[c, x + 1]
            y_prev = jnp.where(is_first_y, below, pltpu.roll(cur, 1, 0))
            y_next = jnp.where(is_last_y, above, pltpu.roll(cur, cy - 1, 0))
            z_prev = jnp.where(is_first_z, 0.0, pltpu.roll(cur, 1, 1))
            z_next = jnp.where(is_last_z, cur, pltpu.roll(cur, nz - 1, 1))
            others = (src[c, x + 2] + (y_prev + y_next)) + (z_prev + z_next)
            return (
                (1.0 - ADVECT - 6.0 * DIFFUSE) * cur
                + (ADVECT + DIFFUSE) * src[c, x]
                + DIFFUSE * others
            )

        def plane_alone(x, carry):
            for c in range(3):
                dst[c, x + 1] = moved(c, x, 0.0, 0.0)
            return carry

        lax.fori_loop(1, split, plane_alone, 0, unroll=UNROLL)

        for copy in part_copies:
            copy.wait_recv()
        whole = []
        for c in range(3):
            total = part_out[n, c]
            for side in range(2):
                other = part_in[n, side, c]
                same, cross = mask_rows[side]
                swapped = jnp.where(first, pltpu.roll(other, ROWS - BLADES, 0), pltpu.roll(other, BLADES, 0))
                total = total + (same * other + cross * swapped)
            whole.append(total)
        if n == 0:
            for copy in lag_copies:
                copy.wait_recv()
            state_rows, rate_rows = [], []
            for e in range(ENTRIES):
                r = jnp.maximum(rotor[e], 0)
                block = lag_g2[r // ny, lax.rem(r, ny)]
                state_rows.append(block[0:BLADES])
                rate_rows.append(block[BLADES : 2 * BLADES])
            lag = jnp.concatenate(state_rows + [zero_rows], axis=0)
            rate = jnp.concatenate(rate_rows + [zero_rows], axis=0)
        cos_b, sin_b = cos_all[n], sin_all[n]
        axial = whole[0]
        tangential = SPIN * radius - (whole[1] * cos_b - whole[2] * sin_b)
        magnitude = jnp.sqrt(axial * axial + tangential * tangential + 1.0)
        lift_static = LIFT_SLOPE * (axial * cos_t - tangential * sin_t) / magnitude
        lag = lag + rate * (lift_static - lag)
        if n == STEPS - 1:
            end_pack[...] = lag
            end_copies = gather_start(1, end_pack, end_g1)
        lift = chord * lag * magnitude
        forces = (-lift * tangential, lift * axial * cos_b, -lift * axial * sin_b)
        for e in range(ENTRIES):
            weighted = []
            for c in range(3):
                weighted.append(
                    jnp.concatenate(
                        [
                            forces[c][BLADES * e + b : BLADES * e + b + 1]
                            * kern_y[n, e, :, b * nz : (b + 1) * nz]
                            for b in range(BLADES)
                        ],
                        axis=1,
                    )
                )
            pushed = lax.dot_general(
                jnp.concatenate(weighted, axis=0),
                kern_z[n, e],
                (((1,), (1,)), ((), ())),
                precision=PRECISE,
                preferred_element_type=jnp.float32,
            )
            spread[n, e] = pushed.reshape(3, cy, nz)
        for copy in halo_copies:
            copy.wait_recv()
        src[:, 0] = jnp.where(gx == 0, inflow_ref[...], halo_x[n, 0])
        src[:, cx + 1] = jnp.where(gx == nx - 1, src[:, cx], halo_x[n, 1])

        def body_force(c, x):
            w0, w1 = weight_x(x - hub_x[0]), weight_x(x - hub_x[1])
            return w0 * spread[n, 0, c] + w1 * spread[n, 1, c]

        def plane_whole(x, carry):
            for c in range(3):
                below, above = halo_rows(c, x)
                dst[c, x + 1] = moved(c, x, below, above) + body_force(c, x)
            return carry

        def plane_rest(x, carry):
            for c in range(3):
                below, above = halo_rows(c, x)
                edge = jnp.where(is_first_y, below, jnp.where(is_last_y, above, 0.0))
                dst[c, x + 1] = dst[c, x + 1] + (body_force(c, x) + DIFFUSE * edge)
            return carry

        def store(k, low, high):
            if n == STEPS - 1:
                copy = pltpu.make_async_copy(
                    dst.at[:, pl.ds(1 + low, high - low)],
                    out_hbm.at[:, pl.ds(low, high - low)],
                    store_sem.at[k],
                )
                copy.start()
                stores.append(copy)

        lax.fori_loop(split, cx - 1, plane_whole, 0, unroll=UNROLL)
        if n == STEPS - 1:
            end_copies = gather_next(1, end_copies, end_g1, end_g2)
        plane_whole(cx - 1, 0)
        store(0, split, cx)
        plane_whole(0, 0)
        half = split // 2
        lax.fori_loop(1, half, plane_rest, 0, unroll=UNROLL)
        store(1, 0, half)
        lax.fori_loop(half, split, plane_rest, 0, unroll=UNROLL)
        store(2, half, split)

    for copy in end_copies:
        copy.wait_recv()
    home_x = pos_ref[0, tile] // cx
    home_y = pos_ref[1, tile] // cy
    block = end_g2[home_x, home_y]
    in_first = cross_ref[0, home_x * ny + home_y] == BLADES * tile
    state_ref[...] = jnp.where(in_first, block[0:BLADES], block[BLADES : 2 * BLADES])
    last = pltpu.make_async_copy(state_ref, state_hbm, small_sem.at[8])
    last.start()
    for copy in started:
        copy.wait_send()
    last.wait()
    for copy in stores:
        copy.wait()


def per_device(
    velocity, inflow, azimuth, positions, crossings, lag_state, lag_rate, chord_len, twist_angle
):
    nx = lax.axis_size("gx")
    ny = lax.axis_size("gy")
    comps, cx, cy, nz = velocity.shape
    own, sections = lag_state.shape
    assert comps == 3 and own == BLADES and sections == nz
    f32 = jnp.float32
    grid = pltpu.VMEM((3, cx + 2, cy, nz), f32)
    dma = pltpu.SemaphoreType.DMA
    hbm = pl.BlockSpec(memory_space=pl.ANY)
    return pl.pallas_call(
        functools.partial(farm_kernel, nx, ny),
        out_shape=(
            jax.ShapeDtypeStruct(velocity.shape, f32),
            jax.ShapeDtypeStruct(lag_state.shape, f32),
        ),
        in_specs=[hbm] * 9,
        out_specs=(hbm, hbm),
        scratch_shapes=[
            pltpu.VMEM(inflow.shape, f32),
            pltpu.SMEM(azimuth.shape, f32),
            pltpu.SMEM(positions.shape[::-1], jnp.int32),
            pltpu.SMEM(crossings.shape[::-1], jnp.int32),
            pltpu.VMEM(lag_state.shape, f32),
            pltpu.VMEM(lag_state.shape, f32),
            pltpu.VMEM((1, sections), f32),
            pltpu.VMEM((1, sections), f32),
            pltpu.VMEM(lag_state.shape, f32),
            dma((9,)),
            grid,
            grid,
            grid,
            pltpu.VMEM((STEPS, 2, 3, cy, nz), f32),
            pltpu.VMEM((STEPS, 2, 3, cx, nz), f32),
            pltpu.VMEM((STEPS, 2, 3, cx, nz), f32),
            pltpu.VMEM((STEPS, 3, ROWS, nz), f32),
            pltpu.VMEM((STEPS, 2, 3, ROWS, nz), f32),
            pltpu.VMEM((STEPS, ENTRIES, cy, BLADES * nz), f32),
            pltpu.VMEM((STEPS, ENTRIES, nz, BLADES * nz), f32),
            pltpu.VMEM((STEPS, ENTRIES, 3, cy, nz), f32),
            pltpu.VMEM((ROWS, nz), f32),
            pltpu.VMEM((ny, ROWS, nz), f32),
            pltpu.VMEM((nx, ny, ROWS, nz), f32),
            pltpu.VMEM((ROWS, nz), f32),
            pltpu.VMEM((ny, ROWS, nz), f32),
            pltpu.VMEM((nx, ny, ROWS, nz), f32),
            dma,
            dma((CHUNKS,)),
            dma((STEPS, 2)),
            dma((STEPS, 2)),
            dma((STEPS, 2)),
            dma((STEPS, 2)),
            dma((STEPS, 2)),
            dma((STEPS, 2)),
            dma((2, ny)),
            dma((2, ny)),
            dma((2, nx)),
            dma((2, nx)),
        ],
        compiler_params=pltpu.CompilerParams(
            collective_id=0, has_side_effects=True, vmem_limit_bytes=60 * 1024 * 1024
        ),
        cost_estimate=pl.CostEstimate(
            flops=50_000_000, bytes_accessed=8 * velocity.size, transcendentals=500_000
        ),
    )(
        velocity,
        inflow,
        azimuth,
        positions.T,
        crossings.T,
        lag_state,
        lag_rate,
        chord_len.reshape(1, sections),
        twist_angle.reshape(1, sections),
    )


def solution(mesh):
    return jax.shard_map(
        per_device,
        mesh=mesh,
        in_specs=(
            P(None, "gx", "gy", None),
            P(None, "gy", None),
            P(),
            P(),
            P(),
            P(("gx", "gy"), None),
            P(("gx", "gy"), None),
            P(),
            P(),
        ),
        out_specs=(P(None, "gx", "gy", None), P(("gx", "gy"), None)),
        check_vma=False,
    )
```

profile of v0, /device:TPU:0, one launch (start us, length us, event | category | flops | bytes accessed | tf_op | source)
XLA Modules:
  0.0 33.0 jit_solution(3960936454713770109)
XLA Ops:
  0.6 27.9 %shard_map.104 = (f32[3,64,32,128]{3,2,1,0:T(8,128)}, f32[3,128]{1,0:T(4,128)}) custom-call(f32[3,64,32,128]{3,2,1,0:T(8,128)} %vel_hbm.1, f32[3,32,128]{2,1,0:T(8,128)} %inflow_hbm.1, f32[32]{0:T(128)} %az_hbm.1, s32[2,32]{1,0:T(2,128)} %bitcast.5, s32[6,32]{1,0:T(8,128)} %bitcast.4, f32[3,128]{1,0:T(4,128)} %lag_hbm.1, f32[3,128]{1,0:T(4,128)} %rate_hbm.1, ...), custom_call_target="tpu_custom_call" | custom-call | flops 50000000 | bytes 6291456 | tf_op jit(solution)/shard_map/pallas_call | solution.py:451
  28.5 0.0 copy-start
  28.5 3.9 %copy.13 = f32[3,64,32,128]{3,2,1,0:T(8,128)} copy(f32[3,64,32,128]{3,2,1,0:T(8,128)} %get-tuple-element.4) | data formatting | bytes 6291456
  32.4 0.0 copy-done
  32.4 0.6 %copy.14 = f32[3,128]{1,0:T(4,128)} copy(f32[3,128]{1,0:T(4,128)S(1)} %copy-done) | data formatting | bytes 3072
Async XLA Ops:
  28.5 3.9 %copy-start = (f32[3,128]{1,0:T(4,128)S(1)}, f32[3,128]{1,0:T(4,128)}, u32[]{:S(2)}) copy-start(f32[3,128]{1,0:T(4,128)} %get-tuple-element.5) | copy-start | bytes 4612
where the time goes:
time: 33.1 us; the launch traced here: 33 us
  Pallas kernels  27.9 us (84%)
  local copies, waits for them, and re-layouts  4.44 us (13%)
  between operations  0.65 us (2%)
    pallas_call x1, Pallas kernels, per_device(): pl.pallas_call(functools.partial(farm_kernel, nx, ny), out_shape=(jax.Sha...  27.9 us
    unnamed x4, local copies, waits for them, and re-layouts  4.44 us

commit v1 on v0

v1 whole, which is shorter than its diff:
```python
import functools
import math

import jax
import jax.numpy as jnp
from jax import lax
from jax.experimental import pallas as pl
from jax.experimental.pallas import tpu as pltpu
from jax.sharding import PartitionSpec as P

RADIUS = 12
HUB = 15
STEPS = 2
EPSILON = 2.0
SUPPORT = 3.0
TURN_RATE = 0.1
SPIN = 0.25
LIFT_SLOPE = 2.0 * math.pi
FORCE_SCALE = 0.15
ADVECT = 0.5
DIFFUSE = 0.05
PRECISE = lax.Precision.HIGH
MESH = pl.DeviceIdType.MESH
BLADES = 3
ENTRIES = 2
ROWS = 8
UNROLL = 4
SLAB = 8
CHUNKS = 4


def taper_const(distance):
    square = distance * distance
    term = max(1.0 - square / (SUPPORT * SUPPORT), 0.0)
    return math.exp(-square / EPSILON**2) * term * term / (EPSILON * math.sqrt(math.pi))


KERN_X = [taper_const(float(i)) for i in range(3)]


def taper_kernel(distance):
    square = distance * distance
    term = jnp.maximum(1.0 - square * (1.0 / (SUPPORT * SUPPORT)), 0.0)
    return (
        jnp.exp(square * (-1.0 / (EPSILON * EPSILON)))
        * (term * term)
        * (1.0 / (EPSILON * math.sqrt(math.pi)))
    )


def weight_x(offset):
    dist = jnp.abs(offset)
    return jnp.where(
        dist == 0,
        KERN_X[0],
        jnp.where(dist == 1, KERN_X[1], jnp.where(dist == 2, KERN_X[2], 0.0)),
    ).astype(jnp.float32)


def farm_kernel(
    nx,
    ny,
    vel_hbm,
    inflow_hbm,
    az_hbm,
    pos_hbm,
    cross_hbm,
    lag_hbm,
    rate_hbm,
    chord_hbm,
    twist_hbm,
    out_ref,
    state_ref,
    inflow_ref,
    az_ref,
    pos_ref,
    cross_ref,
    lag_ref,
    rate_ref,
    chord_ref,
    twist_ref,
    grid0,
    grid1,
    halo_x,
    halo_y,
    face_y,
    part_out,
    part_in,
    kern_y,
    kern_z,
    spread,
    lag_pack,
    lag_in,
    home_out,
    home_in,
    small_sem,
    load_sem,
    hx_send,
    hx_recv,
    hy_send,
    hy_recv,
    ps_send,
    ps_recv,
    lag_send,
    lag_recv,
    home_send,
    home_recv,
):
    f32 = jnp.float32
    _, cx, cy, nz = grid0.shape
    total_y = cy * ny
    devices = nx * ny
    gx = lax.axis_index("gx")
    gy = lax.axis_index("gy")
    tile = gx * ny + gy
    up = lax.rem(gy + 1, ny)
    down = lax.rem(gy + ny - 1, ny)

    def peer(d):
        other = lax.rem(tile + d, devices)
        return (other // ny, lax.rem(other, ny))

    smalls = [
        pltpu.make_async_copy(source, target, small_sem.at[i])
        for i, (source, target) in enumerate(
            (
                (az_hbm, az_ref),
                (pos_hbm, pos_ref),
                (cross_hbm, cross_ref),
                (lag_hbm, lag_ref),
                (rate_hbm, rate_ref),
                (chord_hbm, chord_ref),
                (twist_hbm, twist_ref),
                (inflow_hbm, inflow_ref),
            )
        )
    ]
    for copy in smalls:
        copy.start()
    slabs = [
        pltpu.make_async_copy(vel_hbm.at[:, :, rows], grid0.at[:, :, rows], load_sem.at[i])
        for i, rows in enumerate((pl.ds(cy - SLAB, SLAB), pl.ds(0, SLAB), pl.ds(SLAB, cy - 2 * SLAB)))
    ]
    for copy in slabs:
        copy.start()

    barrier = pltpu.get_barrier_semaphore()

    def greet(d, carry):
        pl.semaphore_signal(barrier, inc=1, device_id=peer(d), device_id_type=MESH)
        return carry

    lax.fori_loop(1, devices, greet, 0)

    for copy in smalls:
        copy.wait()

    rotor, hub_x, load_x, shift_y, valid, az = [], [], [], [], [], []
    for e in range(ENTRIES):
        blade = cross_ref[BLADES * e, tile]
        r = jnp.where(blade >= 0, blade, 0) // BLADES
        rotor.append(jnp.where(blade >= 0, r, -1))
        valid.append(jnp.where(blade >= 0, 1.0, 0.0).astype(f32))
        hub_x.append(jnp.where(blade >= 0, pos_ref[0, r] - gx * cx, 2))
        load_x.append(jnp.clip(hub_x[e], 2, cx - 3))
        off = gy * cy - pos_ref[1, r] + total_y + total_y // 2
        shift_y.append(lax.rem(off, total_y) - total_y // 2)
        az.append(az_ref[r])

    listed = [[cross_ref[BLADES * f, gx * ny + k] for f in range(ENTRIES)] for k in range(ny)]

    def matches(other):
        found = []
        for f in range(ENTRIES):
            blade = cross_ref[BLADES * f, other]
            found.append(jnp.where(blade >= 0, jnp.where(blade >= 0, blade, 0) // BLADES, -2))
        return [
            [jnp.where(rotor[e] == found[f], 1.0, 0.0).astype(f32) for f in range(ENTRIES)]
            for e in range(ENTRIES)
        ]

    row = lax.broadcasted_iota(jnp.int32, (ROWS, nz), 0)
    first = row < BLADES
    lane8 = lax.broadcasted_iota(jnp.int32, (ROWS, nz), 1).astype(f32)
    radius = RADIUS * (lane8 + 0.5) / nz
    spin = jnp.where(first, row, row - BLADES).astype(f32) * (2.0 * math.pi / 3.0)
    base = jnp.where(first, az[0], az[1])
    mask_rows = []
    for other in (gx * ny + down, gx * ny + up):
        m = matches(other)
        mask_rows.append(
            (jnp.where(first, m[0][0], m[1][1]), jnp.where(first, m[0][1], m[1][0]))
        )
    cos_all, sin_all = [], []
    rows_y = lax.broadcasted_iota(jnp.int32, (cy, nz), 0)
    rows_z = lax.broadcasted_iota(jnp.int32, (nz, nz), 0).astype(f32) - HUB
    for n in range(STEPS):
        theta = base + TURN_RATE * n + spin
        cos_n, sin_n = jnp.cos(theta), jnp.sin(theta)
        cos_all.append(cos_n)
        sin_all.append(sin_n)

    def fill_kernels(n):
        rc, rs = radius * cos_all[n], radius * sin_all[n]
        for e in range(ENTRIES):
            y_rel = (rows_y + shift_y[e]).astype(f32)
            for b in range(BLADES):
                i = BLADES * e + b
                kern_y[n, e, :, b * nz : (b + 1) * nz] = taper_kernel(y_rel - rs[i : i + 1]) * valid[e]
                kern_z[n, e, :, b * nz : (b + 1) * nz] = taper_kernel(rows_z - rc[i : i + 1])

    cos_t, sin_t = jnp.cos(twist_ref[...]), jnp.sin(twist_ref[...])
    chord = FORCE_SCALE * chord_ref[...]
    zero_rows = jnp.zeros((ROWS - 2 * BLADES, nz), f32)

    lag_pack[0:BLADES] = lag_ref[...]
    lag_pack[BLADES : 2 * BLADES] = rate_ref[...]
    lag_pack[2 * BLADES : ROWS] = zero_rows
    lag_in[tile] = lag_pack[...]

    started = []

    def send(src, dst, send_sem, recv_sem, axis, other):
        copy = pltpu.make_async_remote_copy(
            src_ref=src,
            dst_ref=dst,
            send_sem=send_sem,
            recv_sem=recv_sem,
            device_id={axis: other},
            device_id_type=MESH,
        )
        copy.start()
        started.append(copy)
        return copy

    def send_lag(d, carry):
        pltpu.make_async_remote_copy(
            src_ref=lag_pack,
            dst_ref=lag_in.at[tile],
            send_sem=lag_send,
            recv_sem=lag_recv,
            device_id=peer(d),
            device_id_type=MESH,
        ).start()
        return carry

    def drain(ref, count, sem):
        block = ref.at[pl.ds(0, count)]
        pltpu.make_async_copy(block, block, sem).wait()

    def sample(n, src):
        cos_n, sin_n = cos_all[n], sin_all[n]
        sampled = [[], [], []]
        for e in range(ENTRIES):
            field = None
            for i in range(-2, 3):
                term = KERN_X[abs(i)] * src[:, load_x[e] + i]
                field = term if field is None else field + term
            inner = jnp.dot(
                field.reshape(3 * cy, nz),
                kern_z[n, e],
                precision=PRECISE,
                preferred_element_type=f32,
            )
            for c in range(3):
                reduced = jnp.sum(inner[c * cy : (c + 1) * cy] * kern_y[n, e], axis=0, keepdims=True)
                sampled[c] += [reduced[:, b * nz : (b + 1) * nz] for b in range(BLADES)]
        s = [jnp.concatenate(sampled[c] + [zero_rows], axis=0) for c in range(3)]
        part_out[n, 0] = s[0]
        part_out[n, 1] = s[1] * cos_n - s[2] * sin_n

    def faces(n, src):
        flat = src.reshape(3 * cx * cy, nz)
        for c in range(3):
            face_y[n, 0, c] = flat[pl.ds(c * cx * cy + cy - 1, cx, stride=cy), :]
            face_y[n, 1, c] = flat[pl.ds(c * cx * cy, cx, stride=cy), :]

    def send_parts(n):
        copies = [
            send(part_out.at[n], part_in.at[n, gy], ps_send.at[n, d], ps_recv.at[n, d], "gy", lax.rem(gy + d, ny))
            for d in range(1, ny)
        ]
        part_in[n, gy] = part_out[n]
        return copies

    def send_faces(n):
        return [
            send(face_y.at[n, 0], halo_y.at[n, 0], hy_send.at[n, 0], hy_recv.at[n, 0], "gy", up),
            send(face_y.at[n, 1], halo_y.at[n, 1], hy_send.at[n, 1], hy_recv.at[n, 1], "gy", down),
        ]

    def x_copies(n, src):
        east = pltpu.make_async_remote_copy(
            src_ref=src.at[:, cx - 1],
            dst_ref=halo_x.at[n, 0],
            send_sem=hx_send.at[n, 0],
            recv_sem=hx_recv.at[n, 0],
            device_id={"gx": lax.rem(gx + 1, nx)},
            device_id_type=MESH,
        )
        west = pltpu.make_async_remote_copy(
            src_ref=src.at[:, 0],
            dst_ref=halo_x.at[n, 1],
            send_sem=hx_send.at[n, 1],
            recv_sem=hx_recv.at[n, 1],
            device_id={"gx": lax.rem(gx + nx - 1, nx)},
            device_id_type=MESH,
        )
        return east, west

    def send_x(n, src):
        east, west = x_copies(n, src)

        @pl.when(gx < nx - 1)
        def _():
            east.start()

        @pl.when(gx > 0)
        def _():
            west.start()

    def wait_x(n, src):
        east, west = x_copies(n, src)

        @pl.when(gx > 0)
        def _():
            east.wait_recv()

        @pl.when(gx == 0)
        def _():
            halo_x[n, 0] = inflow_ref[...]

        @pl.when(gx < nx - 1)
        def _():
            west.wait_recv()

        @pl.when(gx == nx - 1)
        def _():
            halo_x[n, 1] = src[:, cx - 1]

    def wait_x_sent(n, src):
        east, west = x_copies(n, src)

        @pl.when(gx < nx - 1)
        def _():
            east.wait_send()

        @pl.when(gx > 0)
        def _():
            west.wait_send()

    lane = lax.broadcasted_iota(jnp.int32, (cy, nz), 1)
    row_c = lax.broadcasted_iota(jnp.int32, (cy, nz), 0)
    is_first_z, is_last_z = lane == 0, lane == nz - 1
    is_first_y, is_last_y = row_c == 0, row_c == cy - 1

    def moved(cur, prev, following, below, above):
        y_prev = jnp.where(is_first_y, below, pltpu.roll(cur, 1, 0))
        y_next = jnp.where(is_last_y, above, pltpu.roll(cur, cy - 1, 0))
        z_prev = jnp.where(is_first_z, 0.0, pltpu.roll(cur, 1, 1))
        z_next = jnp.where(is_last_z, cur, pltpu.roll(cur, nz - 1, 1))
        others = (following + (y_prev + y_next)) + (z_prev + z_next)
        return (
            (1.0 - ADVECT - 6.0 * DIFFUSE) * cur + (ADVECT + DIFFUSE) * prev + DIFFUSE * others
        )

    def interior(src, dst):
        def plane(x, carry):
            for c in range(3):
                dst[c, x] = moved(src[c, x], src[c, x - 1], src[c, x + 1], 0.0, 0.0)
            return carry

        lax.fori_loop(1, cx - 1, plane, 0, unroll=UNROLL)

    def totals(n):
        whole = []
        for c in range(2):
            total = part_out[n, c]
            for side, other_y in enumerate((down, up)):
                other = part_in[n, other_y, c]
                same, cross = mask_rows[side]
                swapped = jnp.where(first, pltpu.roll(other, ROWS - BLADES, 0), pltpu.roll(other, BLADES, 0))
                total = total + (same * other + cross * swapped)
            whole.append(total)
        return whole

    def relax(lag, rate, axial, turned):
        tangential = SPIN * radius - turned
        magnitude = jnp.sqrt(axial * axial + tangential * tangential + 1.0)
        lift_static = LIFT_SLOPE * (axial * cos_t - tangential * sin_t) / magnitude
        return lag + rate * (lift_static - lag), tangential, magnitude

    def fill_spread(n, lag, axial, tangential, magnitude):
        cos_b, sin_b = cos_all[n], sin_all[n]
        lift = chord * lag * magnitude
        forces = (-lift * tangential, lift * axial * cos_b, -lift * axial * sin_b)
        for e in range(ENTRIES):
            weighted = []
            for c in range(3):
                weighted.append(
                    jnp.concatenate(
                        [
                            forces[c][BLADES * e + b : BLADES * e + b + 1]
                            * kern_y[n, e, :, b * nz : (b + 1) * nz]
                            for b in range(BLADES)
                        ],
                        axis=1,
                    )
                )
            pushed = lax.dot_general(
                jnp.concatenate(weighted, axis=0),
                kern_z[n, e],
                (((1,), (1,)), ((), ())),
                precision=PRECISE,
                preferred_element_type=f32,
            )
            spread[n, e] = pushed.reshape(3, cy, nz)

    def finish(n, src, dst):
        def body_force(c, x):
            w0, w1 = weight_x(x - hub_x[0]), weight_x(x - hub_x[1])
            return w0 * spread[n, 0, c] + w1 * spread[n, 1, c]

        def halo_rows(c, x):
            return halo_y[n, 0, c, pl.ds(x, 1), :], halo_y[n, 1, c, pl.ds(x, 1), :]

        for c in range(3):
            below, above = halo_rows(c, 0)
            dst[c, 0] = moved(src[c, 0], halo_x[n, 0, c], src[c, 1], below, above) + body_force(c, 0)
            x = cx - 1
            below, above = halo_rows(c, x)
            dst[c, x] = moved(src[c, x], src[c, x - 1], halo_x[n, 1, c], below, above) + body_force(c, x)

        def plane_rest(x, carry):
            for c in range(3):
                below, above = halo_rows(c, x)
                edge = jnp.where(is_first_y, below, jnp.where(is_last_y, above, 0.0))
                dst[c, x] = dst[c, x] + (body_force(c, x) + DIFFUSE * edge)
            return carry

        lax.fori_loop(1, cx - 1, plane_rest, 0, unroll=UNROLL)

    def home_blocks(n):
        blocks = []
        for k in range(ny):
            axial, turned = part_in[n, k, 0], part_in[n, k, 1]
            blocks.append(jnp.where(first, axial, pltpu.roll(turned, BLADES, 0)))
            blocks.append(jnp.where(first, pltpu.roll(axial, ROWS - BLADES, 0), turned))
        return blocks

    def fill_home(n):
        blocks = home_blocks(n)
        for h in range(nx):
            wanted = BLADES * (h * ny + gy)
            total = None
            for k in range(ny):
                for f in range(ENTRIES):
                    hit = jnp.where(listed[k][f] == wanted, 1.0, 0.0).astype(f32)
                    term = hit * blocks[ENTRIES * k + f]
                    total = term if total is None else total + term
            home_out[h, n] = total

    fill_kernels(0)
    for copy in slabs:
        copy.wait()
    sample(0, grid0)
    faces(0, grid0)

    pl.semaphore_wait(barrier, devices - 1)
    lax.fori_loop(1, devices, send_lag, 0)
    parts = send_parts(0)
    halos = send_faces(0)
    send_x(0, grid0)
    fill_kernels(1)
    interior(grid0, grid1)
    for copy in parts:
        copy.wait_recv()
    axial, turned = totals(0)
    drain(lag_in, devices - 1, lag_recv)
    state_rows, rate_rows = [], []
    for e in range(ENTRIES):
        block = lag_in[jnp.maximum(rotor[e], 0)]
        state_rows.append(block[0:BLADES])
        rate_rows.append(block[BLADES : 2 * BLADES])
    lag = jnp.concatenate(state_rows + [zero_rows], axis=0)
    rate = jnp.concatenate(rate_rows + [zero_rows], axis=0)
    lag, tangential, magnitude = relax(lag, rate, axial, turned)
    fill_spread(0, lag, axial, tangential, magnitude)
    for copy in halos:
        copy.wait_recv()
    wait_x(0, grid0)
    finish(0, grid0, grid1)

    sample(1, grid1)
    parts = send_parts(1)
    faces(1, grid1)
    halos = send_faces(1)
    send_x(1, grid1)
    fill_home(0)
    interior(grid1, out_ref)
    for copy in parts:
        copy.wait_recv()
    fill_home(1)
    homes = [
        send(
            home_out.at[lax.rem(gx + d, nx)],
            home_in.at[gx],
            home_send.at[d],
            home_recv.at[d],
            "gx",
            lax.rem(gx + d, nx),
        )
        for d in range(1, nx)
    ]
    home_in[gx] = home_out[gx]
    axial, turned = totals(1)
    lag, tangential, magnitude = relax(lag, rate, axial, turned)
    fill_spread(1, lag, axial, tangential, magnitude)
    for copy in halos:
        copy.wait_recv()
    wait_x(1, grid1)
    finish(1, grid1, out_ref)

    for copy in homes:
        copy.wait_recv()
    own = lag_pack[...]
    state, own_rate = own, pltpu.roll(own, ROWS - BLADES, 0)
    for n in range(STEPS):
        total = home_in[0, n]
        for h in range(1, nx):
            total = total + home_in[h, n]
        state, _, _ = relax(state, own_rate, total, pltpu.roll(total, ROWS - BLADES, 0))
    state_ref[...] = state[0:BLADES]
    drain(lag_in, devices - 1, lag_send)
    for n, src in ((0, grid0), (1, grid1)):
        wait_x_sent(n, src)
    for copy in started:
        copy.wait_send()


def store_kernel(vel_ref, state_ref, vel_hbm, state_hbm, sem):
    width = vel_ref.shape[1] // CHUNKS
    copies = [
        pltpu.make_async_copy(
            vel_ref.at[:, pl.ds(i * width, width)], vel_hbm.at[:, pl.ds(i * width, width)], sem.at[i]
        )
        for i in range(CHUNKS)
    ]
    copies.append(pltpu.make_async_copy(state_ref, state_hbm, sem.at[CHUNKS]))
    for copy in copies:
        copy.start()
    for copy in copies:
        copy.wait()


def per_device(
    velocity, inflow, azimuth, positions, crossings, lag_state, lag_rate, chord_len, twist_angle
):
    nx = lax.axis_size("gx")
    ny = lax.axis_size("gy")
    comps, cx, cy, nz = velocity.shape
    own, sections = lag_state.shape
    assert comps == 3 and own == BLADES and sections == nz
    f32 = jnp.float32
    grid = pltpu.VMEM((3, cx, cy, nz), f32)
    dma = pltpu.SemaphoreType.DMA
    hbm = pl.BlockSpec(memory_space=pltpu.HBM)
    vmem = pl.BlockSpec(memory_space=pltpu.VMEM)
    moved, state = pl.pallas_call(
        functools.partial(farm_kernel, nx, ny),
        out_shape=(pltpu.VMEM(velocity.shape, f32), pltpu.VMEM(lag_state.shape, f32)),
        in_specs=[hbm] * 9,
        out_specs=(vmem, vmem),
        scratch_shapes=[
            pltpu.VMEM(inflow.shape, f32),
            pltpu.SMEM(azimuth.shape, f32),
            pltpu.SMEM(positions.shape[::-1], jnp.int32),
            pltpu.SMEM(crossings.shape[::-1], jnp.int32),
            pltpu.VMEM(lag_state.shape, f32),
            pltpu.VMEM(lag_state.shape, f32),
            pltpu.VMEM((1, sections), f32),
            pltpu.VMEM((1, sections), f32),
            grid,
            grid,
            pltpu.VMEM((STEPS, 2, 3, cy, nz), f32),
            pltpu.VMEM((STEPS, 2, 3, cx, nz), f32),
            pltpu.VMEM((STEPS, 2, 3, cx, nz), f32),
            pltpu.VMEM((STEPS, 2, ROWS, nz), f32),
            pltpu.VMEM((STEPS, ny, 2, ROWS, nz), f32),
            pltpu.VMEM((STEPS, ENTRIES, cy, BLADES * nz), f32),
            pltpu.VMEM((STEPS, ENTRIES, nz, BLADES * nz), f32),
            pltpu.VMEM((STEPS, ENTRIES, 3, cy, nz), f32),
            pltpu.VMEM((ROWS, nz), f32),
            pltpu.VMEM((nx * ny, ROWS, nz), f32),
            pltpu.VMEM((nx, STEPS, ROWS, nz), f32),
            pltpu.VMEM((nx, STEPS, ROWS, nz), f32),
            dma((8,)),
            dma((3,)),
            dma((STEPS, 2)),
            dma((STEPS, 2)),
            dma((STEPS, 2)),
            dma((STEPS, 2)),
            dma((STEPS, ny)),
            dma((STEPS, ny)),
            dma,
            dma,
            dma((nx,)),
            dma((nx,)),
        ],
        compiler_params=pltpu.CompilerParams(
            collective_id=0, has_side_effects=True, vmem_limit_bytes=30 * 1024 * 1024
        ),
        cost_estimate=pl.CostEstimate(
            flops=50_000_000, bytes_accessed=8 * velocity.size, transcendentals=500_000
        ),
    )(
        *(
            pltpu.with_memory_space_constraint(source, pltpu.HBM)
            for source in (
                velocity,
                inflow,
                azimuth,
                positions.T,
                crossings.T,
                lag_state,
                lag_rate,
                chord_len.reshape(1, sections),
                twist_angle.reshape(1, sections),
            )
        )
    )
    anywhere = pl.BlockSpec(memory_space=pl.ANY)
    return pl.pallas_call(
        store_kernel,
        out_shape=(
            jax.ShapeDtypeStruct(velocity.shape, f32),
            jax.ShapeDtypeStruct(lag_state.shape, f32),
        ),
        in_specs=[anywhere] * 2,
        out_specs=(pl.BlockSpec(memory_space=pltpu.HBM),) * 2,
        scratch_shapes=[dma((CHUNKS + 1,))],
        compiler_params=pltpu.CompilerParams(vmem_limit_bytes=16 * 1024 * 1024),
    )(
        pltpu.with_memory_space_constraint(moved, pltpu.VMEM),
        pltpu.with_memory_space_constraint(state, pltpu.VMEM),
    )


def solution(mesh):
    return jax.shard_map(
        per_device,
        mesh=mesh,
        in_specs=(
            P(None, "gx", "gy", None),
            P(None, "gy", None),
            P(),
            P(),
            P(),
            P(("gx", "gy"), None),
            P(("gx", "gy"), None),
            P(),
            P(),
        ),
        out_specs=(P(None, "gx", "gy", None), P(("gx", "gy"), None)),
        check_vma=False,
    )
```

time: 33.1 us -> 28.2 us (0.85)
  local copies, waits for them, and re-layouts: 4.44 us -> 0 us
  Pallas kernels: 27.9 us -> 27.4 us
    unnamed x4 -> x0, local copies, waits for them, and re-layouts: 4.44 us -> none
    pallas_call x1 -> x2, Pallas kernels: 27.9 us -> 27.4 us  [the longest x1 25.7 us: per_device(): pl.pallas_call(functools.partial(farm_kernel, nx, ny), out_shape=(pltpu.V...]
where the time goes in v1:
time: 28.2 us; the launch traced here: 28 us
  Pallas kernels  27.4 us (97%)
  between operations  0.64 us (2%)
    pallas_call x1, Pallas kernels, per_device(): pl.pallas_call(functools.partial(farm_kernel, nx, ny), out_shape=(pltpu.V...  25.7 us
    pallas_call x1, Pallas kernels, per_device(): pl.pallas_call(store_kernel, out_shape=(jax.ShapeDtypeStruct(velocity.sha...  1.7 us

profile of v1, /device:TPU:0, one launch (start us, length us, event | category | flops | bytes accessed | tf_op | source)
XLA Modules:
  0.0 28.0 jit_solution(15557479487706669434)
XLA Ops:
  0.6 25.7 %shard_map.104 = (f32[3,64,32,128]{3,2,1,0:T(8,128)S(1)}, f32[3,128]{1,0:T(4,128)S(1)}) custom-call(f32[3,64,32,128]{3,2,1,0:T(8,128)} %vel_hbm.1, f32[3,32,128]{2,1,0:T(8,128)} %inflow_hbm.1, f32[32]{0:T(128)} %az_hbm.1, s32[2,32]{1,0:T(2,128)} %bitcast.5, s32[6,32]{1,0:T(8,128)} %bitcast.4, f32[3,128]{1,0:T(4,128)} %lag_hbm.1, f32[3,128]{1,0:T(4,128)} %rate_hbm.1, ...), custom_call_target="tpu_custom_call" | custom-call | flops 50000000 | bytes 6291456 | tf_op jit(solution)/shard_map/pallas_call | solution.py:569
  26.3 1.7 %shard_map.105 = (f32[3,64,32,128]{3,2,1,0:T(8,128)}, f32[3,128]{1,0:T(4,128)}) custom-call(f32[3,64,32,128]{3,2,1,0:T(8,128)S(1)} %get-tuple-element.4.vel_ref, f32[3,128]{1,0:T(4,128)S(1)} %get-tuple-element.5.state_ref), custom_call_target="tpu_custom_call" | custom-call | tf_op jit(solution)/shard_map/pallas_call | solution.py:633

commit v2 on v1

--- a/solution.py
+++ b/solution.py
@@ -90,7 +90,10 @@
     kern_z,
     spread,
     lag_pack,
+    lag_col,
     lag_in,
+    rows_out,
+    rows_in,
     home_out,
     home_in,
     small_sem,
@@ -101,24 +104,23 @@
     hy_recv,
     ps_send,
     ps_recv,
-    lag_send,
-    lag_recv,
+    ly_send,
+    ly_recv,
+    lx_send,
+    lx_recv,
+    rw_send,
+    rw_recv,
     home_send,
     home_recv,
 ):
     f32 = jnp.float32
     _, cx, cy, nz = grid0.shape
     total_y = cy * ny
-    devices = nx * ny
     gx = lax.axis_index("gx")
     gy = lax.axis_index("gy")
     tile = gx * ny + gy
     up = lax.rem(gy + 1, ny)
     down = lax.rem(gy + ny - 1, ny)
-
-    def peer(d):
-        other = lax.rem(tile + d, devices)
-        return (other // ny, lax.rem(other, ny))
 
     smalls = [
         pltpu.make_async_copy(source, target, small_sem.at[i])
@@ -146,11 +148,14 @@
 
     barrier = pltpu.get_barrier_semaphore()
 
-    def greet(d, carry):
-        pl.semaphore_signal(barrier, inc=1, device_id=peer(d), device_id_type=MESH)
-        return carry
-
-    lax.fori_loop(1, devices, greet, 0)
+    for d in range(1, ny):
+        pl.semaphore_signal(
+            barrier, inc=1, device_id={"gy": lax.rem(gy + d, ny)}, device_id_type=MESH
+        )
+    for d in range(1, nx):
+        pl.semaphore_signal(
+            barrier, inc=1, device_id={"gx": lax.rem(gx + d, nx)}, device_id_type=MESH
+        )
 
     for copy in smalls:
         copy.wait()
@@ -216,7 +221,6 @@
     lag_pack[0:BLADES] = lag_ref[...]
     lag_pack[BLADES : 2 * BLADES] = rate_ref[...]
     lag_pack[2 * BLADES : ROWS] = zero_rows
-    lag_in[tile] = lag_pack[...]
 
     started = []
 
@@ -233,20 +237,21 @@
         started.append(copy)
         return copy
 
-    def send_lag(d, carry):
-        pltpu.make_async_remote_copy(
-            src_ref=lag_pack,
-            dst_ref=lag_in.at[tile],
-            send_sem=lag_send,
-            recv_sem=lag_recv,
-            device_id=peer(d),
-            device_id_type=MESH,
-        ).start()
-        return carry
-
-    def drain(ref, count, sem):
-        block = ref.at[pl.ds(0, count)]
-        pltpu.make_async_copy(block, block, sem).wait()
+    def send_lag_column():
+        copies = [
+            send(lag_pack, lag_col.at[gy], ly_send.at[d], ly_recv.at[d], "gy", lax.rem(gy + d, ny))
+            for d in range(1, ny)
+        ]
+        lag_col[gy] = lag_pack[...]
+        return copies
+
+    def send_lag_block():
+        copies = [
+            send(lag_col, lag_in.at[gx], lx_send.at[d], lx_recv.at[d], "gx", lax.rem(gx + d, nx))
+            for d in range(1, nx)
+        ]
+        lag_in[gx] = lag_col[...]
+        return copies
 
     def sample(n, src):
         cos_n, sin_n = cos_all[n], sin_all[n]
@@ -370,7 +375,11 @@
                 dst[c, x] = moved(src[c, x], src[c, x - 1], src[c, x + 1], 0.0, 0.0)
             return carry
 
+        for c in range(3):
+            dst[c, 0] = moved(src[c, 0], 0.0, src[c, 1], 0.0, 0.0)
         lax.fori_loop(1, cx - 1, plane, 0, unroll=UNROLL)
+        for c in range(3):
+            dst[c, cx - 1] = moved(src[c, cx - 1], src[c, cx - 2], 0.0, 0.0, 0.0)
 
     def totals(n):
         whole = []
@@ -416,20 +425,13 @@
             )
             spread[n, e] = pushed.reshape(3, cy, nz)
 
-    def finish(n, src, dst):
+    def finish(n, dst):
         def body_force(c, x):
             w0, w1 = weight_x(x - hub_x[0]), weight_x(x - hub_x[1])
             return w0 * spread[n, 0, c] + w1 * spread[n, 1, c]
 
         def halo_rows(c, x):
             return halo_y[n, 0, c, pl.ds(x, 1), :], halo_y[n, 1, c, pl.ds(x, 1), :]
-
-        for c in range(3):
-            below, above = halo_rows(c, 0)
-            dst[c, 0] = moved(src[c, 0], halo_x[n, 0, c], src[c, 1], below, above) + body_force(c, 0)
-            x = cx - 1
-            below, above = halo_rows(c, x)
-            dst[c, x] = moved(src[c, x], src[c, x - 1], halo_x[n, 1, c], below, above) + body_force(c, x)
 
         def plane_rest(x, carry):
             for c in range(3):
@@ -438,7 +440,39 @@
                 dst[c, x] = dst[c, x] + (body_force(c, x) + DIFFUSE * edge)
             return carry
 
-        lax.fori_loop(1, cx - 1, plane_rest, 0, unroll=UNROLL)
+        lax.fori_loop(0, cx, plane_rest, 0, unroll=UNROLL)
+        for c in range(3):
+            dst[c, 0] = dst[c, 0] + (ADVECT + DIFFUSE) * halo_x[n, 0, c]
+            dst[c, cx - 1] = dst[c, cx - 1] + DIFFUSE * halo_x[n, 1, c]
+
+    def send_rows():
+        for side, edge in enumerate((cy - 1, 0)):
+            for c in range(3):
+                for e in range(ENTRIES):
+                    rows_out[side, c, e : e + 1] = spread[0, e, c, edge : edge + 1]
+                for k in range(2):
+                    rows_out[side, c, 2 + k : 3 + k] = halo_x[0, k, c, edge : edge + 1]
+        return [
+            send(rows_out.at[0], rows_in.at[0], rw_send.at[0], rw_recv.at[0], "gy", up),
+            send(rows_out.at[1], rows_in.at[1], rw_send.at[1], rw_recv.at[1], "gy", down),
+        ]
+
+    def complete_halo():
+        plane_id = lax.broadcasted_iota(jnp.int32, (cx, nz), 0)
+        at_low = jnp.where(plane_id == 0, ADVECT + DIFFUSE, 0.0).astype(f32)
+        at_high = jnp.where(plane_id == cx - 1, DIFFUSE, 0.0).astype(f32)
+        for side, other in enumerate((down, up)):
+            weights = []
+            for f in range(ENTRIES):
+                blade = cross_ref[BLADES * f, gx * ny + other]
+                r = jnp.where(blade >= 0, blade, 0) // BLADES
+                weights.append(weight_x(plane_id - (pos_ref[0, r] - gx * cx)))
+            weights += [at_low, at_high]
+            for c in range(3):
+                total = halo_y[1, side, c] + DIFFUSE * face_y[0, 1 - side, c]
+                for k in range(4):
+                    total = total + weights[k] * rows_in[side, c, k : k + 1]
+                halo_y[1, side, c] = total
 
     def home_blocks(n):
         blocks = []
@@ -466,35 +500,41 @@
     sample(0, grid0)
     faces(0, grid0)
 
-    pl.semaphore_wait(barrier, devices - 1)
-    lax.fori_loop(1, devices, send_lag, 0)
+    pl.semaphore_wait(barrier, nx - 1 + ny - 1)
+    lags = send_lag_column()
     parts = send_parts(0)
     halos = send_faces(0)
     send_x(0, grid0)
+    interior(grid0, grid1)
+    faces(1, grid1)
+    late_halos = send_faces(1)
     fill_kernels(1)
-    interior(grid0, grid1)
+    for copy in lags:
+        copy.wait_recv()
+    lags = send_lag_block()
     for copy in parts:
         copy.wait_recv()
     axial, turned = totals(0)
-    drain(lag_in, devices - 1, lag_recv)
+    for copy in lags:
+        copy.wait_recv()
     state_rows, rate_rows = [], []
     for e in range(ENTRIES):
-        block = lag_in[jnp.maximum(rotor[e], 0)]
+        r = jnp.maximum(rotor[e], 0)
+        block = lag_in[r // ny, lax.rem(r, ny)]
         state_rows.append(block[0:BLADES])
         rate_rows.append(block[BLADES : 2 * BLADES])
     lag = jnp.concatenate(state_rows + [zero_rows], axis=0)
     rate = jnp.concatenate(rate_rows + [zero_rows], axis=0)
     lag, tangential, magnitude = relax(lag, rate, axial, turned)
     fill_spread(0, lag, axial, tangential, magnitude)
+    wait_x(0, grid0)
+    rows = send_rows()
     for copy in halos:
         copy.wait_recv()
-    wait_x(0, grid0)
-    finish(0, grid0, grid1)
+    finish(0, grid1)
 
     sample(1, grid1)
     parts = send_parts(1)
-    faces(1, grid1)
-    halos = send_faces(1)
     send_x(1, grid1)
     fill_home(0)
     interior(grid1, out_ref)
@@ -516,10 +556,11 @@
     axial, turned = totals(1)
     lag, tangential, magnitude = relax(lag, rate, axial, turned)
     fill_spread(1, lag, axial, tangential, magnitude)
-    for copy in halos:
+    wait_x(1, grid1)
+    for copy in rows + late_halos:
         copy.wait_recv()
-    wait_x(1, grid1)
-    finish(1, grid1, out_ref)
+    complete_halo()
+    finish(1, out_ref)
 
     for copy in homes:
         copy.wait_recv()
@@ -531,7 +572,6 @@
             total = total + home_in[h, n]
         state, _, _ = relax(state, own_rate, total, pltpu.roll(total, ROWS - BLADES, 0))
     state_ref[...] = state[0:BLADES]
-    drain(lag_in, devices - 1, lag_send)
     for n, src in ((0, grid0), (1, grid1)):
         wait_x_sent(n, src)
     for copy in started:
@@ -591,7 +631,10 @@
             pltpu.VMEM((STEPS, ENTRIES, nz, BLADES * nz), f32),
             pltpu.VMEM((STEPS, ENTRIES, 3, cy, nz), f32),
             pltpu.VMEM((ROWS, nz), f32),
-            pltpu.VMEM((nx * ny, ROWS, nz), f32),
+            pltpu.VMEM((ny, ROWS, nz), f32),
+            pltpu.VMEM((nx, ny, ROWS, nz), f32),
+            pltpu.VMEM((2, 3, 4, nz), f32),
+            pltpu.VMEM((2, 3, 4, nz), f32),
             pltpu.VMEM((nx, STEPS, ROWS, nz), f32),
             pltpu.VMEM((nx, STEPS, ROWS, nz), f32),
             dma((8,)),
@@ -602,8 +645,12 @@
             dma((STEPS, 2)),
             dma((STEPS, ny)),
             dma((STEPS, ny)),
-            dma,
-            dma,
+            dma((ny,)),
+            dma((ny,)),
+            dma((nx,)),
+            dma((nx,)),
+            dma((2,)),
+            dma((2,)),
             dma((nx,)),
             dma((nx,)),
         ],

time: 28.2 us -> 25.7 us (0.911)
  Pallas kernels: 27.4 us -> 24.9 us
    pallas_call x1, Pallas kernels: 25.7 us -> 23.2 us  [per_device(): pl.pallas_call(functools.partial(farm_kernel, nx, ny), out_shape=(pltpu.V...]
where the time goes in v2:
time: 25.7 us; the launch traced here: 25.5 us
  Pallas kernels  24.9 us (97%)
  between operations  0.64 us (2%)
    pallas_call x1, Pallas kernels, per_device(): pl.pallas_call(functools.partial(farm_kernel, nx, ny), out_shape=(pltpu.V...  23.2 us
    pallas_call x1, Pallas kernels, per_device(): pl.pallas_call(store_kernel, out_shape=(jax.ShapeDtypeStruct(velocity.sha...  1.7 us

profile of v2, /device:TPU:0, one launch (start us, length us, event | category | flops | bytes accessed | tf_op | source)
XLA Modules:
  0.0 25.5 jit_solution(2927045034681561281)
XLA Ops:
  0.6 23.2 %shard_map.104 = (f32[3,64,32,128]{3,2,1,0:T(8,128)S(1)}, f32[3,128]{1,0:T(4,128)S(1)}) custom-call(f32[3,64,32,128]{3,2,1,0:T(8,128)} %vel_hbm.1, f32[3,32,128]{2,1,0:T(8,128)} %inflow_hbm.1, f32[32]{0:T(128)} %az_hbm.1, s32[2,32]{1,0:T(2,128)} %bitcast.5, s32[6,32]{1,0:T(8,128)} %bitcast.4, f32[3,128]{1,0:T(4,128)} %lag_hbm.1, f32[3,128]{1,0:T(4,128)} %rate_hbm.1, ...), custom_call_target="tpu_custom_call" | custom-call | flops 50000000 | bytes 6291456 | tf_op jit(solution)/shard_map/pallas_call | solution.py:609
  23.8 1.7 %shard_map.105 = (f32[3,64,32,128]{3,2,1,0:T(8,128)}, f32[3,128]{1,0:T(4,128)}) custom-call(f32[3,64,32,128]{3,2,1,0:T(8,128)S(1)} %get-tuple-element.4.vel_ref, f32[3,128]{1,0:T(4,128)S(1)} %get-tuple-element.5.state_ref), custom_call_target="tpu_custom_call" | custom-call | tf_op jit(solution)/shard_map/pallas_call | solution.py:680

commit v3 on v2

--- a/solution.py
+++ b/solution.py
@@ -21,6 +21,9 @@
 DIFFUSE = 0.05
 PRECISE = lax.Precision.HIGH
 MESH = pl.DeviceIdType.MESH
+CENTRE = round((1.0 - ADVECT - 6.0 * DIFFUSE) / DIFFUSE)
+LEAD = (ADVECT + DIFFUSE) / DIFFUSE
+GROUP = 16
 BLADES = 3
 ENTRIES = 2
 ROWS = 8
@@ -36,6 +39,9 @@
 
 
 KERN_X = [taper_const(float(i)) for i in range(3)]
+PAIR_X = [
+    sum(KERN_X[abs(i)] * KERN_X[abs(i + d)] for i in range(-2, 3) if abs(i + d) <= 2) for d in range(5)
+]
 
 
 def taper_kernel(distance):
@@ -55,6 +61,14 @@
         KERN_X[0],
         jnp.where(dist == 1, KERN_X[1], jnp.where(dist == 2, KERN_X[2], 0.0)),
     ).astype(jnp.float32)
+
+
+def pair_x(offset):
+    dist = jnp.abs(offset)
+    total = jnp.where(dist == 0, PAIR_X[0], 0.0)
+    for d in range(1, 5):
+        total = jnp.where(dist == d, PAIR_X[d], total)
+    return total.astype(jnp.float32)
 
 
 def farm_kernel(
@@ -83,6 +97,7 @@
     grid1,
     halo_x,
     halo_y,
+    late_y,
     face_y,
     part_out,
     part_in,
@@ -253,16 +268,18 @@
         lag_in[gx] = lag_col[...]
         return copies
 
-    def sample(n, src):
-        cos_n, sin_n = cos_all[n], sin_all[n]
+    def plane_sum(src, e):
+        field = None
+        for i in range(-2, 3):
+            term = KERN_X[abs(i)] * src[:, load_x[e] + i]
+            field = term if field is None else field + term
+        return field
+
+    def sample(n, fields):
         sampled = [[], [], []]
         for e in range(ENTRIES):
-            field = None
-            for i in range(-2, 3):
-                term = KERN_X[abs(i)] * src[:, load_x[e] + i]
-                field = term if field is None else field + term
             inner = jnp.dot(
-                field.reshape(3 * cy, nz),
+                fields[e].reshape(3 * cy, nz),
                 kern_z[n, e],
                 precision=PRECISE,
                 preferred_element_type=f32,
@@ -271,8 +288,28 @@
                 reduced = jnp.sum(inner[c * cy : (c + 1) * cy] * kern_y[n, e], axis=0, keepdims=True)
                 sampled[c] += [reduced[:, b * nz : (b + 1) * nz] for b in range(BLADES)]
         s = [jnp.concatenate(sampled[c] + [zero_rows], axis=0) for c in range(3)]
-        part_out[n, 0] = s[0]
-        part_out[n, 1] = s[1] * cos_n - s[2] * sin_n
+        return s[0], s[1] * cos_all[n] - s[2] * sin_all[n]
+
+    def late_fields():
+        fields = []
+        for e in range(ENTRIES):
+            pair = [pair_x(hub_x[e] - hub_x[f]) for f in range(ENTRIES)]
+            low = jnp.where(hub_x[e] == 2, KERN_X[2] * (ADVECT + DIFFUSE), 0.0).astype(f32)
+            high = jnp.where(hub_x[e] == cx - 3, KERN_X[2] * DIFFUSE, 0.0).astype(f32)
+            planes = []
+            for c in range(3):
+                rows = []
+                for side in range(2):
+                    total = None
+                    for i in range(-2, 3):
+                        term = (DIFFUSE * KERN_X[abs(i)]) * halo_y[side, c, pl.ds(load_x[e] + i, 1), :]
+                        total = term if total is None else total + term
+                    rows.append(total)
+                edge = jnp.where(is_first_y, rows[0], jnp.where(is_last_y, rows[1], 0.0))
+                force = pair[0] * spread[0, 0, c] + pair[1] * spread[0, 1, c]
+                planes.append((force + edge) + (low * halo_x[0, 0, c] + high * halo_x[0, 1, c]))
+            fields.append(jnp.stack(planes))
+        return fields
 
     def faces(n, src):
         flat = src.reshape(3 * cx * cy, nz)
@@ -288,10 +325,10 @@
         part_in[n, gy] = part_out[n]
         return copies
 
-    def send_faces(n):
+    def send_faces(n, target):
         return [
-            send(face_y.at[n, 0], halo_y.at[n, 0], hy_send.at[n, 0], hy_recv.at[n, 0], "gy", up),
-            send(face_y.at[n, 1], halo_y.at[n, 1], hy_send.at[n, 1], hy_recv.at[n, 1], "gy", down),
+            send(face_y.at[n, 0], target.at[0], hy_send.at[n, 0], hy_recv.at[n, 0], "gy", up),
+            send(face_y.at[n, 1], target.at[1], hy_send.at[n, 1], hy_recv.at[n, 1], "gy", down),
         ]
 
     def x_copies(n, src):
@@ -354,32 +391,43 @@
         def _():
             west.wait_send()
 
-    lane = lax.broadcasted_iota(jnp.int32, (cy, nz), 1)
     row_c = lax.broadcasted_iota(jnp.int32, (cy, nz), 0)
-    is_first_z, is_last_z = lane == 0, lane == nz - 1
     is_first_y, is_last_y = row_c == 0, row_c == cy - 1
 
-    def moved(cur, prev, following, below, above):
-        y_prev = jnp.where(is_first_y, below, pltpu.roll(cur, 1, 0))
-        y_next = jnp.where(is_last_y, above, pltpu.roll(cur, cy - 1, 0))
-        z_prev = jnp.where(is_first_z, 0.0, pltpu.roll(cur, 1, 1))
-        z_next = jnp.where(is_last_z, cur, pltpu.roll(cur, nz - 1, 1))
-        others = (following + (y_prev + y_next)) + (z_prev + z_next)
-        return (
-            (1.0 - ADVECT - 6.0 * DIFFUSE) * cur + (ADVECT + DIFFUSE) * prev + DIFFUSE * others
-        )
-
     def interior(src, dst):
-        def plane(x, carry):
+        group = min(GROUP, cx)
+        zi = lax.broadcasted_iota(jnp.int32, (2 * nz, nz), 0)
+        zi = jnp.where(zi >= nz, zi - nz, zi)
+        zo = lax.broadcasted_iota(jnp.int32, (2 * nz, nz), 1)
+        near = jnp.where(jnp.abs(zi - zo) == 1, 1.0, 0.0) + jnp.where(zi == zo, CENTRE, 0.0)
+        near = near + jnp.where((zi == zo) & (zo == nz - 1), 1.0, 0.0)
+        near = near.astype(jnp.bfloat16)
+
+        def planes(k, carry):
+            x0 = pl.multiple_of(k * group, group)
             for c in range(3):
-                dst[c, x] = moved(src[c, x], src[c, x - 1], src[c, x + 1], 0.0, 0.0)
+                cur = src[c, pl.ds(x0, group)].reshape(group * cy, nz)
+                high = cur.astype(jnp.bfloat16)
+                low = (cur - high.astype(f32)).astype(jnp.bfloat16)
+                z_near = jnp.dot(jnp.concatenate([high, low], axis=1), near, preferred_element_type=f32)
+                for g in range(group):
+                    x = x0 + g
+                    own = src[c, x]
+                    y_prev = jnp.where(is_first_y, 0.0, pltpu.roll(own, 1, 0))
+                    y_next = jnp.where(is_last_y, 0.0, pltpu.roll(own, cy - 1, 0))
+                    total = z_near[g * cy : (g + 1) * cy] + (y_prev + y_next)
+                    if g == 0:
+                        total = total + jnp.where(x0 > 0, LEAD, 0.0) * src[c, jnp.maximum(x - 1, 0)]
+                    else:
+                        total = total + LEAD * src[c, x - 1]
+                    if g == group - 1:
+                        total = total + jnp.where(x0 < cx - group, 1.0, 0.0) * src[c, jnp.minimum(x + 1, cx - 1)]
+                    else:
+                        total = total + src[c, x + 1]
+                    dst[c, x] = DIFFUSE * total
             return carry
 
-        for c in range(3):
-            dst[c, 0] = moved(src[c, 0], 0.0, src[c, 1], 0.0, 0.0)
-        lax.fori_loop(1, cx - 1, plane, 0, unroll=UNROLL)
-        for c in range(3):
-            dst[c, cx - 1] = moved(src[c, cx - 1], src[c, cx - 2], 0.0, 0.0, 0.0)
+        lax.fori_loop(0, cx // group, planes, 0)
 
     def totals(n):
         whole = []
@@ -431,7 +479,8 @@
             return w0 * spread[n, 0, c] + w1 * spread[n, 1, c]
 
         def halo_rows(c, x):
-            return halo_y[n, 0, c, pl.ds(x, 1), :], halo_y[n, 1, c, pl.ds(x, 1), :]
+            ref = (halo_y, late_y)[n]
+            return ref[0, c, pl.ds(x, 1), :], ref[1, c, pl.ds(x, 1), :]
 
         def plane_rest(x, carry):
             for c in range(3):
@@ -469,10 +518,10 @@
                 weights.append(weight_x(plane_id - (pos_ref[0, r] - gx * cx)))
             weights += [at_low, at_high]
             for c in range(3):
-                total = halo_y[1, side, c] + DIFFUSE * face_y[0, 1 - side, c]
+                total = late_y[side, c] + DIFFUSE * face_y[0, 1 - side, c]
                 for k in range(4):
                     total = total + weights[k] * rows_in[side, c, k : k + 1]
-                halo_y[1, side, c] = total
+                late_y[side, c] = total
 
     def home_blocks(n):
         blocks = []
@@ -494,24 +543,24 @@
                     total = term if total is None else total + term
             home_out[h, n] = total
 
-    fill_kernels(0)
-    for copy in slabs:
-        copy.wait()
-    sample(0, grid0)
-    faces(0, grid0)
-
     pl.semaphore_wait(barrier, nx - 1 + ny - 1)
     lags = send_lag_column()
+    for copy in slabs[:2]:
+        copy.wait()
+    faces(0, grid0)
+    halos = send_faces(0, halo_y)
+    slabs[2].wait()
+    send_x(0, grid0)
+    fill_kernels(0)
+    part_out[0, 0], part_out[0, 1] = sample(0, [plane_sum(grid0, e) for e in range(ENTRIES)])
     parts = send_parts(0)
-    halos = send_faces(0)
-    send_x(0, grid0)
     interior(grid0, grid1)
     faces(1, grid1)
-    late_halos = send_faces(1)
-    fill_kernels(1)
     for copy in lags:
         copy.wait_recv()
     lags = send_lag_block()
+    fill_kernels(1)
+    early = sample(1, [plane_sum(grid1, e) for e in range(ENTRIES)])
     for copy in parts:
         copy.wait_recv()
     axial, turned = totals(0)
@@ -528,13 +577,15 @@
     lag, tangential, magnitude = relax(lag, rate, axial, turned)
     fill_spread(0, lag, axial, tangential, magnitude)
     wait_x(0, grid0)
-    rows = send_rows()
     for copy in halos:
         copy.wait_recv()
+    late = sample(1, late_fields())
+    for c in range(2):
+        part_out[1, c] = early[c] + late[c]
+    parts = send_parts(1)
+    rows = send_rows()
+    late_halos = send_faces(1, late_y)
     finish(0, grid1)
-
-    sample(1, grid1)
-    parts = send_parts(1)
     send_x(1, grid1)
     fill_home(0)
     interior(grid1, out_ref)
@@ -623,7 +674,8 @@
             grid,
             grid,
             pltpu.VMEM((STEPS, 2, 3, cy, nz), f32),
-            pltpu.VMEM((STEPS, 2, 3, cx, nz), f32),
+            pltpu.VMEM((2, 3, cx, nz), f32),
+            pltpu.VMEM((2, 3, cx, nz), f32),
             pltpu.VMEM((STEPS, 2, 3, cx, nz), f32),
             pltpu.VMEM((STEPS, 2, ROWS, nz), f32),
             pltpu.VMEM((STEPS, ny, 2, ROWS, nz), f32),

time: 25.7 us -> 24.4 us (0.949)
  Pallas kernels: 24.9 us -> 23.6 us
    pallas_call x1, Pallas kernels: 23.2 us -> 21.9 us  [per_device(): pl.pallas_call(functools.partial(farm_kernel, nx, ny), out_shape=(pltpu.V...]
where the time goes in v3:
time: 24.4 us; the launch traced here: 24.2 us
  Pallas kernels  23.6 us (97%)
  between operations  0.64 us (3%)
    pallas_call x1, Pallas kernels, per_device(): pl.pallas_call(functools.partial(farm_kernel, nx, ny), out_shape=(pltpu.V...  21.9 us
    pallas_call x1, Pallas kernels, per_device(): pl.pallas_call(store_kernel, out_shape=(jax.ShapeDtypeStruct(velocity.sha...  1.7 us

profile of v3, /device:TPU:0, one launch (start us, length us, event | category | flops | bytes accessed | tf_op | source)
XLA Modules:
  0.0 24.2 jit_solution(10107358981629489513)
XLA Ops:
  0.6 21.9 %shard_map.104 = (f32[3,64,32,128]{3,2,1,0:T(8,128)S(1)}, f32[3,128]{1,0:T(4,128)S(1)}) custom-call(f32[3,64,32,128]{3,2,1,0:T(8,128)} %vel_hbm.1, f32[3,32,128]{2,1,0:T(8,128)} %inflow_hbm.1, f32[32]{0:T(128)} %az_hbm.1, s32[2,32]{1,0:T(2,128)} %bitcast.5, s32[6,32]{1,0:T(8,128)} %bitcast.4, f32[3,128]{1,0:T(4,128)} %lag_hbm.1, f32[3,128]{1,0:T(4,128)} %rate_hbm.1, ...), custom_call_target="tpu_custom_call" | custom-call | flops 50000000 | bytes 6291456 | tf_op jit(solution)/shard_map/pallas_call | solution.py:660
  22.5 1.7 %shard_map.105 = (f32[3,64,32,128]{3,2,1,0:T(8,128)}, f32[3,128]{1,0:T(4,128)}) custom-call(f32[3,64,32,128]{3,2,1,0:T(8,128)S(1)} %get-tuple-element.4.vel_ref, f32[3,128]{1,0:T(4,128)S(1)} %get-tuple-element.5.state_ref), custom_call_target="tpu_custom_call" | custom-call | tf_op jit(solution)/shard_map/pallas_call | solution.py:732

commit v4 on v3

--- a/solution.py
+++ b/solution.py
@@ -106,9 +106,12 @@
     spread,
     lag_pack,
     lag_col,
+    lag_out,
     lag_in,
     rows_out,
     rows_in,
+    edge_out,
+    edge_in,
     home_out,
     home_in,
     small_sem,
@@ -125,6 +128,8 @@
     lx_recv,
     rw_send,
     rw_recv,
+    ed_send,
+    ed_recv,
     home_send,
     home_recv,
 ):
@@ -141,11 +146,11 @@
         pltpu.make_async_copy(source, target, small_sem.at[i])
         for i, (source, target) in enumerate(
             (
+                (lag_hbm, lag_ref),
+                (rate_hbm, rate_ref),
                 (az_hbm, az_ref),
                 (pos_hbm, pos_ref),
                 (cross_hbm, cross_ref),
-                (lag_hbm, lag_ref),
-                (rate_hbm, rate_ref),
                 (chord_hbm, chord_ref),
                 (twist_hbm, twist_ref),
                 (inflow_hbm, inflow_ref),
@@ -172,7 +177,38 @@
             barrier, inc=1, device_id={"gx": lax.rem(gx + d, nx)}, device_id_type=MESH
         )
 
-    for copy in smalls:
+    for copy in smalls[:2]:
+        copy.wait()
+    zero_rows = jnp.zeros((ROWS - 2 * BLADES, nz), f32)
+    lag_pack[0:BLADES] = lag_ref[...]
+    lag_pack[BLADES : 2 * BLADES] = rate_ref[...]
+    lag_pack[2 * BLADES : ROWS] = zero_rows
+    started = []
+
+    def send(src, dst, send_sem, recv_sem, axis, other):
+        copy = pltpu.make_async_remote_copy(
+            src_ref=src,
+            dst_ref=dst,
+            send_sem=send_sem,
+            recv_sem=recv_sem,
+            device_id={axis: other},
+            device_id_type=MESH,
+        )
+        copy.start()
+        started.append(copy)
+        return copy
+
+    def send_lag_column():
+        copies = [
+            send(lag_pack, lag_col.at[gy], ly_send.at[d], ly_recv.at[d], "gy", lax.rem(gy + d, ny))
+            for d in range(1, ny)
+        ]
+        lag_col[gy] = lag_pack[...]
+        return copies
+
+    pl.semaphore_wait(barrier, nx - 1 + ny - 1)
+    lags = send_lag_column()
+    for copy in smalls[2:]:
         copy.wait()
 
     rotor, hub_x, load_x, shift_y, valid, az = [], [], [], [], [], []
@@ -231,41 +267,19 @@
 
     cos_t, sin_t = jnp.cos(twist_ref[...]), jnp.sin(twist_ref[...])
     chord = FORCE_SCALE * chord_ref[...]
-    zero_rows = jnp.zeros((ROWS - 2 * BLADES, nz), f32)
-
-    lag_pack[0:BLADES] = lag_ref[...]
-    lag_pack[BLADES : 2 * BLADES] = rate_ref[...]
-    lag_pack[2 * BLADES : ROWS] = zero_rows
-
-    started = []
-
-    def send(src, dst, send_sem, recv_sem, axis, other):
-        copy = pltpu.make_async_remote_copy(
-            src_ref=src,
-            dst_ref=dst,
-            send_sem=send_sem,
-            recv_sem=recv_sem,
-            device_id={axis: other},
-            device_id_type=MESH,
-        )
-        copy.start()
-        started.append(copy)
-        return copy
-
-    def send_lag_column():
-        copies = [
-            send(lag_pack, lag_col.at[gy], ly_send.at[d], ly_recv.at[d], "gy", lax.rem(gy + d, ny))
-            for d in range(1, ny)
-        ]
-        lag_col[gy] = lag_pack[...]
-        return copies
+
 
     def send_lag_block():
-        copies = [
-            send(lag_col, lag_in.at[gx], lx_send.at[d], lx_recv.at[d], "gx", lax.rem(gx + d, nx))
-            for d in range(1, nx)
-        ]
-        lag_in[gx] = lag_col[...]
+        for h in range(nx):
+            for f in range(ENTRIES):
+                blade = cross_ref[BLADES * f, h * ny + gy]
+                r = jnp.where(blade >= 0, blade, 0) // BLADES
+                lag_out[h, f] = lag_col[lax.rem(r, ny)]
+        copies = []
+        for d in range(1, nx):
+            other = lax.rem(gx + d, nx)
+            copies.append(send(lag_out.at[other], lag_in.at[gx], lx_send.at[d], lx_recv.at[d], "gx", other))
+        lag_in[gx] = lag_out[gx]
         return copies
 
     def plane_sum(src, e):
@@ -298,13 +312,8 @@
             high = jnp.where(hub_x[e] == cx - 3, KERN_X[2] * DIFFUSE, 0.0).astype(f32)
             planes = []
             for c in range(3):
-                rows = []
-                for side in range(2):
-                    total = None
-                    for i in range(-2, 3):
-                        term = (DIFFUSE * KERN_X[abs(i)]) * halo_y[side, c, pl.ds(load_x[e] + i, 1), :]
-                        total = term if total is None else total + term
-                    rows.append(total)
+                k = 3 * e + c
+                rows = [edge_in[side, k : k + 1] for side in range(2)]
                 edge = jnp.where(is_first_y, rows[0], jnp.where(is_last_y, rows[1], 0.0))
                 force = pair[0] * spread[0, 0, c] + pair[1] * spread[0, 1, c]
                 planes.append((force + edge) + (low * halo_x[0, 0, c] + high * halo_x[0, 1, c]))
@@ -329,6 +338,25 @@
         return [
             send(face_y.at[n, 0], target.at[0], hy_send.at[n, 0], hy_recv.at[n, 0], "gy", up),
             send(face_y.at[n, 1], target.at[1], hy_send.at[n, 1], hy_recv.at[n, 1], "gy", down),
+        ]
+
+    def send_edges():
+        for side, other in enumerate((up, down)):
+            for f in range(ENTRIES):
+                blade = cross_ref[BLADES * f, gx * ny + other]
+                r = jnp.where(blade >= 0, blade, 0) // BLADES
+                centre = jnp.where(blade >= 0, jnp.clip(pos_ref[0, r] - gx * cx, 2, cx - 3), 2)
+                for c in range(3):
+                    total = None
+                    for i in range(-2, 3):
+                        term = (DIFFUSE * KERN_X[abs(i)]) * face_y[0, side, c, pl.ds(centre + i, 1), :]
+                        total = term if total is None else total + term
+                    k = 3 * f + c
+                    edge_out[side, k : k + 1] = total
+            edge_out[side, 3 * ENTRIES : ROWS] = zero_rows
+        return [
+            send(edge_out.at[0], edge_in.at[0], ed_send.at[0], ed_recv.at[0], "gy", up),
+            send(edge_out.at[1], edge_in.at[1], ed_send.at[1], ed_recv.at[1], "gy", down),
         ]
 
     def x_copies(n, src):
@@ -473,26 +501,36 @@
             )
             spread[n, e] = pushed.reshape(3, cy, nz)
 
-    def finish(n, dst):
-        def body_force(c, x):
+    def push(n, dst):
+        def plane(x, carry):
             w0, w1 = weight_x(x - hub_x[0]), weight_x(x - hub_x[1])
-            return w0 * spread[n, 0, c] + w1 * spread[n, 1, c]
-
-        def halo_rows(c, x):
-            ref = (halo_y, late_y)[n]
-            return ref[0, c, pl.ds(x, 1), :], ref[1, c, pl.ds(x, 1), :]
-
-        def plane_rest(x, carry):
             for c in range(3):
-                below, above = halo_rows(c, x)
-                edge = jnp.where(is_first_y, below, jnp.where(is_last_y, above, 0.0))
-                dst[c, x] = dst[c, x] + (body_force(c, x) + DIFFUSE * edge)
+                dst[c, x] = dst[c, x] + (w0 * spread[n, 0, c] + w1 * spread[n, 1, c])
             return carry
 
-        lax.fori_loop(0, cx, plane_rest, 0, unroll=UNROLL)
+        lax.fori_loop(0, cx, plane, 0, unroll=UNROLL)
+
+    def add_x(n, dst):
         for c in range(3):
             dst[c, 0] = dst[c, 0] + (ADVECT + DIFFUSE) * halo_x[n, 0, c]
             dst[c, cx - 1] = dst[c, cx - 1] + DIFFUSE * halo_x[n, 1, c]
+
+    row_s = lax.broadcasted_iota(jnp.int32, (SLAB, nz), 0)
+    is_low, is_high = row_s == 0, row_s == SLAB - 1
+
+    def add_y(n, dst):
+        def plane(x, carry):
+            at = pl.ds(x, 1)
+            for c in range(3):
+                below, above = halo_y[0, c, at, :], halo_y[1, c, at, :]
+                if n == 1:
+                    below, above = below + late_y[0, c, at, :], above + late_y[1, c, at, :]
+                low, high = pl.ds(0, SLAB), pl.ds(cy - SLAB, SLAB)
+                dst[c, x, low] = dst[c, x, low] + jnp.where(is_low, DIFFUSE * below, 0.0)
+                dst[c, x, high] = dst[c, x, high] + jnp.where(is_high, DIFFUSE * above, 0.0)
+            return carry
+
+        lax.fori_loop(0, cx, plane, 0, unroll=2 * UNROLL)
 
     def send_rows():
         for side, edge in enumerate((cy - 1, 0)):
@@ -518,10 +556,10 @@
                 weights.append(weight_x(plane_id - (pos_ref[0, r] - gx * cx)))
             weights += [at_low, at_high]
             for c in range(3):
-                total = late_y[side, c] + DIFFUSE * face_y[0, 1 - side, c]
+                total = DIFFUSE * face_y[0, 1 - side, c]
                 for k in range(4):
                     total = total + weights[k] * rows_in[side, c, k : k + 1]
-                late_y[side, c] = total
+                halo_y[side, c] = total
 
     def home_blocks(n):
         blocks = []
@@ -543,17 +581,15 @@
                     total = term if total is None else total + term
             home_out[h, n] = total
 
-    pl.semaphore_wait(barrier, nx - 1 + ny - 1)
-    lags = send_lag_column()
-    for copy in slabs[:2]:
+    fill_kernels(0)
+    for copy in slabs:
         copy.wait()
-    faces(0, grid0)
-    halos = send_faces(0, halo_y)
-    slabs[2].wait()
-    send_x(0, grid0)
-    fill_kernels(0)
     part_out[0, 0], part_out[0, 1] = sample(0, [plane_sum(grid0, e) for e in range(ENTRIES)])
     parts = send_parts(0)
+    faces(0, grid0)
+    edges = send_edges()
+    halos = send_faces(0, halo_y)
+    send_x(0, grid0)
     interior(grid0, grid1)
     faces(1, grid1)
     for copy in lags:
@@ -569,7 +605,7 @@
     state_rows, rate_rows = [], []
     for e in range(ENTRIES):
         r = jnp.maximum(rotor[e], 0)
-        block = lag_in[r // ny, lax.rem(r, ny)]
+        block = lag_in[r // ny, e]
         state_rows.append(block[0:BLADES])
         rate_rows.append(block[BLADES : 2 * BLADES])
     lag = jnp.concatenate(state_rows + [zero_rows], axis=0)
@@ -577,7 +613,7 @@
     lag, tangential, magnitude = relax(lag, rate, axial, turned)
     fill_spread(0, lag, axial, tangential, magnitude)
     wait_x(0, grid0)
-    for copy in halos:
+    for copy in edges:
         copy.wait_recv()
     late = sample(1, late_fields())
     for c in range(2):
@@ -585,7 +621,11 @@
     parts = send_parts(1)
     rows = send_rows()
     late_halos = send_faces(1, late_y)
-    finish(0, grid1)
+    for copy in halos:
+        copy.wait_recv()
+    push(0, grid1)
+    add_x(0, grid1)
+    add_y(0, grid1)
     send_x(1, grid1)
     fill_home(0)
     interior(grid1, out_ref)
@@ -607,11 +647,15 @@
     axial, turned = totals(1)
     lag, tangential, magnitude = relax(lag, rate, axial, turned)
     fill_spread(1, lag, axial, tangential, magnitude)
-    wait_x(1, grid1)
-    for copy in rows + late_halos:
+    push(1, out_ref)
+    for copy in rows:
         copy.wait_recv()
     complete_halo()
-    finish(1, out_ref)
+    wait_x(1, grid1)
+    add_x(1, out_ref)
+    for copy in late_halos:
+        copy.wait_recv()
+    add_y(1, out_ref)
 
     for copy in homes:
         copy.wait_recv()
@@ -684,9 +728,12 @@
             pltpu.VMEM((STEPS, ENTRIES, 3, cy, nz), f32),
             pltpu.VMEM((ROWS, nz), f32),
             pltpu.VMEM((ny, ROWS, nz), f32),
-            pltpu.VMEM((nx, ny, ROWS, nz), f32),
+            pltpu.VMEM((nx, ENTRIES, ROWS, nz), f32),
+            pltpu.VMEM((nx, ENTRIES, ROWS, nz), f32),
             pltpu.VMEM((2, 3, 4, nz), f32),
             pltpu.VMEM((2, 3, 4, nz), f32),
+            pltpu.VMEM((2, ROWS, nz), f32),
+            pltpu.VMEM((2, ROWS, nz), f32),
             pltpu.VMEM((nx, STEPS, ROWS, nz), f32),
             pltpu.VMEM((nx, STEPS, ROWS, nz), f32),
             dma((8,)),
@@ -701,6 +748,8 @@
             dma((ny,)),
             dma((nx,)),
             dma((nx,)),
+            dma((2,)),
+            dma((2,)),
             dma((2,)),
             dma((2,)),
             dma((nx,)),

time: 24.4 us -> 23.8 us (0.975)
  Pallas kernels: 23.6 us -> 23 us
    pallas_call x1, Pallas kernels: 21.9 us -> 21.3 us  [per_device(): pl.pallas_call(functools.partial(farm_kernel, nx, ny), out_shape=(pltpu.V...]
where the time goes in v4:
time: 23.8 us; the launch traced here: 23.6 us
  Pallas kernels  23 us (97%)
  between operations  0.64 us (3%)
    pallas_call x1, Pallas kernels, per_device(): pl.pallas_call(functools.partial(farm_kernel, nx, ny), out_shape=(pltpu.V...  21.3 us
    pallas_call x1, Pallas kernels, per_device(): pl.pallas_call(store_kernel, out_shape=(jax.ShapeDtypeStruct(velocity.sha...  1.7 us

profile of v4, /device:TPU:0, one launch (start us, length us, event | category | flops | bytes accessed | tf_op | source)
XLA Modules:
  0.0 23.6 jit_solution(2328654631401690028)
XLA Ops:
  0.6 21.3 %shard_map.104 = (f32[3,64,32,128]{3,2,1,0:T(8,128)S(1)}, f32[3,128]{1,0:T(4,128)S(1)}) custom-call(f32[3,64,32,128]{3,2,1,0:T(8,128)} %vel_hbm.1, f32[3,32,128]{2,1,0:T(8,128)} %inflow_hbm.1, f32[32]{0:T(128)} %az_hbm.1, s32[2,32]{1,0:T(2,128)} %bitcast.5, s32[6,32]{1,0:T(8,128)} %bitcast.4, f32[3,128]{1,0:T(4,128)} %lag_hbm.1, f32[3,128]{1,0:T(4,128)} %rate_hbm.1, ...), custom_call_target="tpu_custom_call" | custom-call | flops 50000000 | bytes 6291456 | tf_op jit(solution)/shard_map/pallas_call | solution.py:704
  21.9 1.7 %shard_map.105 = (f32[3,64,32,128]{3,2,1,0:T(8,128)}, f32[3,128]{1,0:T(4,128)}) custom-call(f32[3,64,32,128]{3,2,1,0:T(8,128)S(1)} %get-tuple-element.4.vel_ref, f32[3,128]{1,0:T(4,128)S(1)} %get-tuple-element.5.state_ref), custom_call_target="tpu_custom_call" | custom-call | tf_op jit(solution)/shard_map/pallas_call | solution.py:781
